TPU v7x, 512 devices: a whole 4x8x8 slice. The times are simulated.
512 devices in a mesh: rows: 128 (over y, x, z_hi), chan: 4 (over z_lo, core).
Axes of the slice: x: 4, y: 8, z: 8 (z_hi: 4, z_lo: 2; z = z_hi * 2 + z_lo), core: 2. Of those that a mesh axis runs over, the one named last changes fastest.
Arguments:
- field: float32 [64, 1024, 1024], P('chan', 'rows'), may hold values from -6 to 6
- weights: bfloat16 [2, 64, 64, 65536], P(None, None, None, ('rows', 'chan')), may hold values from -0.5 to 0.5
- cotangent: float32 [64, 512, 512], P('chan', 'rows'), may hold values from -6 to 6
Outputs:
- grad_field: bfloat16 [64, 1024, 1024], P('chan', 'rows')
- grad_weights: bfloat16 [2, 64, 64, 65536], P(None, None, None, ('rows', 'chan'))
All inputs are finite; a program needn't handle non-finite values.
Results may differ from a plain program's by a relative error of at most 0.0012.
Values sent between devices are 32-bit elements; how exact they have to be, the bound alone decides.
A program may use at most 64 MiB of HBM per device.

v0:
```python
import functools
import math

import jax
import jax.numpy as jnp
import ml_dtypes
import numpy as np
from jax import lax
from jax.experimental import pallas as pl
from jax.experimental.pallas import tpu as pltpu
from jax.sharding import PartitionSpec as P

MESH = pl.DeviceIdType.MESH
ROWS = 128
CHANS = 4
KW = 256
KH = 256
W = 1024
H = 1024
GH = 512
GW = 512
HL = H // ROWS
TL = GH // ROWS
FAR_FIRST = sorted(
    ((dy, dx, dz) for dx in (2, 1, 3, 0) for dz in (2, 1, 3, 0) for dy in (4, 3, 5, 2, 6, 1, 7, 0) if (dy, dx, dz) != (0, 0, 0)),
    key=lambda o: -(min(o[0], 8 - o[0]) + min(o[1], 4 - o[1]) + 2 * min(o[2], 4 - o[2])),
)
NT = (((1,), (1,)), ((), ()))
NN = (((1,), (0,)), ((), ()))


def split_table(table):
    high = table.astype(np.float32).astype(ml_dtypes.bfloat16)
    low = (table - high.astype(np.float64)).astype(np.float32).astype(ml_dtypes.bfloat16)
    return high, low


def wave(first, second, length):
    angle = (first[:, None] * second[None, :]) % length * (2.0 * math.pi / length)
    return np.cos(angle), np.sin(angle)


def tables():
    dev = np.arange(ROWS)
    freq = np.arange(KH) - KH // 2
    fine, coarse = [], []
    for k in range(2):
        c, s = wave(2 * dev + k, np.arange(W), W)
        fine += [c / math.sqrt(W), -s / math.sqrt(W)]
        c, s = wave(2 * dev + k, np.arange(GW), GW)
        coarse += [c / math.sqrt(KH * KW), -s / math.sqrt(KH * KW)]
    tall, short = [], []
    for h in range(HL):
        c, s = wave(HL * dev + h, freq, H)
        tall.append(np.concatenate([c, s], 1) / math.sqrt(H))
    for t in range(TL):
        c, s = wave(TL * dev + t, freq, GH)
        short.append(np.concatenate([c, s], 1))
    out = []
    for parts in (fine, tall, short, coarse):
        out += split_table(np.concatenate(parts, 0))
    return out


def halves(value):
    high = value.astype(jnp.bfloat16)
    return high, (value - high.astype(jnp.float32)).astype(jnp.bfloat16)


def dot3(a, b, dims):
    def one(x, y):
        return lax.dot_general(x, y, dims, preferred_element_type=jnp.float32)

    return one(a[0], b[1]) + one(a[1], b[0]) + one(a[0], b[0])


def gelu_slope(values):
    cdf = 0.5 * (1.0 + lax.erf(values * (1.0 / math.sqrt(2.0))))
    pdf = jnp.exp(-0.5 * values * values) * (1.0 / math.sqrt(2.0 * math.pi))
    return cdf + values * pdf


def kernel(
    field_hbm, weights_hbm, cot_hbm, fine_h, fine_l, tall_h, tall_l, short_h, short_l, coarse_h, coarse_l,
    gfield_hbm, gweights_hbm,
    field, weights, cot, t1h, t1l, t2h, t2l, t3h, t3l, t4h, t4l, gfield, gweights,
    send1, recv1, send2, recv2, send3, recv3, send4, recv4,
    csend, crecv, turned, mixed, modes_r, modes_i, slope_r, slope_i, back_r, back_i,
    in_sem, out_sem, row_send, row_recv, chan_send, chan_recv,
):
    me = lax.axis_index("rows")
    mc = lax.axis_index("chan")
    me_y, me_x, me_z = me // 16, lax.rem(me // 4, 4), lax.rem(me, 4)

    barrier = pltpu.get_barrier_semaphore()

    def greet(k, _):
        pl.semaphore_signal(barrier, inc=1, device_id={"rows": lax.rem(me + k, ROWS)}, device_id_type=MESH)
        return 0

    lax.fori_loop(1, ROWS, greet, 0, unroll=8)
    for k in range(1, CHANS):
        pl.semaphore_signal(barrier, inc=1, device_id={"chan": lax.rem(mc + k, CHANS)}, device_id_type=MESH)

    loads = [
        pltpu.make_async_copy(src, dst, in_sem.at[n])
        for n, (src, dst) in enumerate(
            [
                (field_hbm, field), (fine_h, t1h), (fine_l, t1l), (tall_h, t2h), (tall_l, t2l),
                (weights_hbm, weights), (short_h, t3h), (short_l, t3l), (coarse_h, t4h), (coarse_l, t4l),
                (cot_hbm, cot),
            ]
        )
    ]
    for load in loads:
        load.start()

    def spread_rows(send, recv, n):
        for dy, dx, dz in FAR_FIRST:
            d = lax.rem(me_y + dy, 8) * 16 + lax.rem(me_x + dx, 4) * 4 + lax.rem(me_z + dz, 4)
            pltpu.make_async_remote_copy(
                src_ref=send.at[d], dst_ref=recv.at[me], send_sem=row_send.at[n], recv_sem=row_recv.at[n],
                device_id={"rows": d}, device_id_type=MESH,
            ).start()
        recv[me] = send[me]

    def await_rows(recv, n):
        part = recv.at[pl.ds(0, ROWS - 1)]
        pltpu.make_async_copy(part, part, row_recv.at[n]).wait()

    def spread_chans(n):
        for k in range(1, CHANS):
            d = lax.rem(mc + k, CHANS)
            pltpu.make_async_remote_copy(
                src_ref=csend.at[n, d], dst_ref=crecv.at[n, mc], send_sem=chan_send.at[n], recv_sem=chan_recv.at[n],
                device_id={"chan": d}, device_id_type=MESH,
            ).start()
        crecv[n, mc] = csend[n, mc]

    def await_chans(n):
        part = crecv.at[n, pl.ds(0, CHANS - 1)]
        pltpu.make_async_copy(part, part, chan_recv.at[n]).wait()

    def to_modes(product, n):
        for k in range(2):
            re, im = product[32 * k : 32 * k + 16], product[32 * k + 16 : 32 * k + 32]
            real = re[:, :KH] + im[:, KH:]
            imag = im[:, :KH] - re[:, KH:]
            for j in range(2):
                csend[n, 2 * k + j, 0:16, :] = real[:, 128 * j : 128 * j + 128]
                csend[n, 2 * k + j, 16:32, :] = imag[:, 128 * j : 128 * j + 128]
        spread_chans(n)

    def own_modes(n, real, imag):
        for s in range(CHANS):
            real[16 * s : 16 * s + 16, :] = crecv[n, s, 0:16, :]
            imag[16 * s : 16 * s + 16, :] = crecv[n, s, 16:32, :]

    def from_modes(n):
        rows = []
        for k in range(2):
            real = jnp.concatenate([crecv[n, 2 * k, 0:16, :], crecv[n, 2 * k + 1, 0:16, :]], axis=1)
            imag = jnp.concatenate([crecv[n, 2 * k, 16:32, :], crecv[n, 2 * k + 1, 16:32, :]], axis=1)
            rows.append(jnp.concatenate([real, -imag], axis=1))
            rows.append(jnp.concatenate([imag, real], axis=1))
        return halves(jnp.concatenate(rows, axis=0))

    def give_modes(n, real, imag):
        for d in range(CHANS):
            csend[n, d, 0:16, :] = real[16 * d : 16 * d + 16, :]
            csend[n, d, 16:32, :] = imag[16 * d : 16 * d + 16, :]
        spread_chans(n)

    for n in (0, 1, 2):
        loads[n].wait()
    fine = (t1h[...], t1l[...])
    spectra = dot3(fine, halves(field[...]), NT)
    for s in range(4):
        send1[:, s, :] = spectra[128 * s : 128 * s + 128]
    pl.semaphore_wait(barrier, ROWS - 1 + CHANS - 1)
    spread_rows(send1, recv1, 0)
    for n in range(3, 11):
        loads[n].wait()
    await_rows(recv1, 0)

    for s in range(4):
        turned[s] = recv1[:, s, :].T
    left = jnp.concatenate(
        [
            jnp.concatenate([turned[s, pl.ds(h, 16, stride=HL), :] for h in range(HL)], axis=1)
            for s in range(4)
        ],
        axis=0,
    )
    to_modes(dot3(halves(left), (t2h[...], t2l[...]), NN), 0)
    await_chans(0)
    own_modes(0, modes_r, modes_i)

    def mix(i, carry):
        out_r, out_i = carry
        xr, xi = modes_r[pl.ds(i, 1), :], modes_i[pl.ds(i, 1), :]
        wr, wi = weights[0, i].astype(jnp.float32), weights[1, i].astype(jnp.float32)
        return out_r + xr * wr - xi * wi, out_i + xr * wi + xi * wr

    zero = jnp.zeros((64, 128), jnp.float32)
    out_r, out_i = lax.fori_loop(0, 64, mix, (zero, zero), unroll=4)
    give_modes(1, out_r, out_i)
    await_chans(1)

    rows_t = dot3((t3h[...], t3l[...]), from_modes(1), NT)
    for s in range(2):
        send2[:, s, :] = jnp.concatenate([rows_t[256 * s : 256 * s + 128], rows_t[256 * s + 128 : 256 * s + 256]], axis=1)
    spread_rows(send2, recv2, 1)
    await_rows(recv2, 1)
    rows = []
    for s in range(2):
        turn = recv2[:, s, :].T
        for t in range(2):
            rows.append(jnp.concatenate([turn[64 * t + 16 * u : 64 * t + 16 * u + 16] for u in range(4)], axis=1))
    coarse = (t4h[...], t4l[...])
    values = dot3(halves(jnp.concatenate(rows, axis=0)), coarse, NN)
    cotangent = jnp.concatenate([cot[:, t, :] for t in range(TL)], axis=0)
    grad_v = cotangent * gelu_slope(values)

    cols_t = dot3(coarse, halves(grad_v), NT)
    for s in range(2):
        send3[:, s, :] = jnp.concatenate([cols_t[256 * s : 256 * s + 128], cols_t[256 * s + 128 : 256 * s + 256]], axis=1)
    spread_rows(send3, recv3, 2)
    await_rows(recv3, 2)
    rows = []
    for s in range(2):
        turn = recv3[:, s, :].T
        for p in range(2):
            rows.append(jnp.concatenate([turn[64 * p + 16 * u : 64 * p + 16 * u + 16] for u in range(4)], axis=1))
    to_modes(dot3(halves(jnp.concatenate(rows, axis=0)), (t3h[...], t3l[...]), NN), 2)
    await_chans(2)
    own_modes(2, slope_r, slope_i)

    def unmix(i, _):
        gr, gi = slope_r[...], slope_i[...]
        wr, wi = weights[0, i].astype(jnp.float32), weights[1, i].astype(jnp.float32)
        back_r[pl.ds(i, 1), :] = jnp.sum(wr * gr + wi * gi, axis=0, keepdims=True)
        back_i[pl.ds(i, 1), :] = jnp.sum(wr * gi - wi * gr, axis=0, keepdims=True)
        return 0

    lax.fori_loop(0, 64, unmix, 0, unroll=4)
    give_modes(3, back_r, back_i)

    def outer(i, _):
        gr, gi = slope_r[...], slope_i[...]
        xr, xi = modes_r[pl.ds(i, 1), :], modes_i[pl.ds(i, 1), :]
        gweights[0, i] = (xr * gr + xi * gi).astype(jnp.bfloat16)
        gweights[1, i] = (xr * gi - xi * gr).astype(jnp.bfloat16)
        return 0

    await_chans(3)

    fine_t = dot3((t2h[...], t2l[...]), from_modes(3), NT)
    for s in range(4):
        send4[:, s, :] = jnp.concatenate([fine_t[256 * s : 256 * s + 128], fine_t[256 * s + 128 : 256 * s + 256]], axis=1)
    spread_rows(send4, recv4, 3)
    lax.fori_loop(0, 64, outer, 0, unroll=4)
    store = pltpu.make_async_copy(gweights, gweights_hbm, out_sem.at[0])
    store.start()
    await_rows(recv4, 3)
    for s in range(4):
        turn = recv4[:, s, :].T
        for h in range(2):
            for u in range(4):
                mixed[u, pl.ds(2 * s + h, 16, stride=HL), :] = turn[64 * h + 16 * u : 64 * h + 16 * u + 16]
    left = jnp.concatenate([mixed[u] for u in range(4)], axis=1)
    gfield[...] = dot3(halves(left), (t1h[...], t1l[...]), NN)
    last = pltpu.make_async_copy(gfield, gfield_hbm, out_sem.at[1])
    last.start()
    for n, send in enumerate((send1, send2, send3, send4)):
        part = send.at[pl.ds(0, ROWS - 1)]
        pltpu.make_async_copy(part, part, row_send.at[n]).wait()
    for n in range(4):
        part = csend.at[n, pl.ds(0, CHANS - 1)]
        pltpu.make_async_copy(part, part, chan_send.at[n]).wait()
    store.wait()
    last.wait()


def local(field, weights, cotangent):
    consts = [jnp.asarray(t) for t in tables()]
    f32, bf16 = jnp.float32, jnp.bfloat16
    anywhere = pl.BlockSpec(memory_space=pl.ANY)
    gfield, gweights = pl.pallas_call(
        kernel,
        out_shape=(
            jax.ShapeDtypeStruct((128, W), f32),
            jax.ShapeDtypeStruct(weights.shape, bf16),
        ),
        in_specs=[anywhere] * 11,
        out_specs=(anywhere, anywhere),
        scratch_shapes=[
            pltpu.VMEM((128, W), f32),
            pltpu.VMEM(weights.shape, bf16),
            pltpu.VMEM(cotangent.shape, f32),
            *[pltpu.VMEM(t.shape, bf16) for t in consts],
            pltpu.VMEM((128, W), f32),
            pltpu.VMEM(weights.shape, bf16),
            *[pltpu.VMEM((ROWS, n, 128), f32) for n in (4, 4, 2, 2, 2, 2, 4, 4)],
            pltpu.VMEM((4, CHANS, 32, 128), f32),
            pltpu.VMEM((4, CHANS, 32, 128), f32),
            pltpu.VMEM((4, 128, 128), f32),
            pltpu.VMEM((4, 128, 128), f32),
            *[pltpu.VMEM((64, 128), f32)] * 6,
            pltpu.SemaphoreType.DMA((11,)),
            pltpu.SemaphoreType.DMA((2,)),
            pltpu.SemaphoreType.DMA((4,)),
            pltpu.SemaphoreType.DMA((4,)),
            pltpu.SemaphoreType.DMA((4,)),
            pltpu.SemaphoreType.DMA((4,)),
        ],
        compiler_params=pltpu.CompilerParams(
            collective_id=0, has_side_effects=True, vmem_limit_bytes=48 * 2**20
        ),
    )(field.reshape(128, W), weights, cotangent, *consts)
    return gfield.astype(bf16).reshape(field.shape), gweights


def solution(mesh):
    spread = P("chan", "rows", None)
    by_mode = P(None, None, None, ("rows", "chan"))
    return jax.shard_map(
        local, mesh=mesh, in_specs=(spread, by_mode, spread), out_specs=(spread, by_mode), check_vma=False
    )
```

profile of v0, /device:TPU:1, one launch (start us, length us, event | category | flops | bytes accessed | tf_op | source)
XLA Modules:
  0.0 87.4 jit_solution(44142485555197057)
XLA Ops:
  0.6 0.0 copy-start
  0.6 1.2 %copy-done = bf16[512,1024]{1,0:T(8,128)(2,1)S(1)} copy-done((bf16[512,1024]{1,0:T(8,128)(2,1)S(1)}, bf16[512,1024]{1,0:T(8,128)(2,1)}, u32[]{:S(2)}) %copy-start) | copy-done | bytes 1048600
  1.9 0.0 copy-start.1
  1.9 1.2 %copy-done.1 = bf16[512,1024]{1,0:T(8,128)(2,1)S(1)} copy-done((bf16[512,1024]{1,0:T(8,128)(2,1)S(1)}, bf16[512,1024]{1,0:T(8,128)(2,1)}, u32[]{:S(2)}) %copy-start.1) | copy-done | bytes 1048600
  3.1 0.0 copy-start.2
  3.1 1.0 %copy-done.2 = f32[16,8,1024]{2,1,0:T(8,128)S(1)} copy-done((f32[16,8,1024]{2,1,0:T(8,128)S(1)}, f32[16,8,1024]{2,1,0:T(8,128)}, u32[]{:S(2)}) %copy-start.2) | copy-done | bytes 524312
  4.1 0.0 copy-start.3
  4.1 1.0 %copy-done.3 = bf16[512,512]{1,0:T(8,128)(2,1)S(1)} copy-done((bf16[512,512]{1,0:T(8,128)(2,1)S(1)}, bf16[512,512]{1,0:T(8,128)(2,1)}, u32[]{:S(2)}) %copy-start.3) | copy-done | bytes 524312
  5.2 0.0 copy-start.4
  5.2 1.0 %copy-done.4 = bf16[512,512]{1,0:T(8,128)(2,1)S(1)} copy-done((bf16[512,512]{1,0:T(8,128)(2,1)S(1)}, bf16[512,512]{1,0:T(8,128)(2,1)}, u32[]{:S(2)}) %copy-start.4) | copy-done | bytes 524312
  6.2 0.0 copy-start.5
  6.2 1.0 %copy-done.5 = bf16[512,512]{1,0:T(8,128)(2,1)S(1)} copy-done((bf16[512,512]{1,0:T(8,128)(2,1)S(1)}, bf16[512,512]{1,0:T(8,128)(2,1)}, u32[]{:S(2)}) %copy-start.5) | copy-done | bytes 524312
  7.3 0.0 copy-start.6
  7.3 1.0 %copy-done.6 = bf16[512,512]{1,0:T(8,128)(2,1)S(1)} copy-done((bf16[512,512]{1,0:T(8,128)(2,1)S(1)}, bf16[512,512]{1,0:T(8,128)(2,1)}, u32[]{:S(2)}) %copy-start.6) | copy-done | bytes 524312
  8.3 0.0 copy-start.7
  8.3 0.9 %copy-done.7 = f32[16,4,512]{2,1,0:T(4,128)S(1)} copy-done((f32[16,4,512]{2,1,0:T(4,128)S(1)}, f32[16,4,512]{2,1,0:T(4,128)}, u32[]{:S(2)}) %copy-start.7) | copy-done | bytes 131096
  9.2 74.4 %shard_map.122 = (f32[128,1024]{1,0:T(8,128)S(1)}, bf16[2,64,64,128]{3,2,1,0:T(8,128)(2,1)}) custom-call(f32[128,1024]{1,0:T(8,128)S(1)} %bitcast.3, bf16[2,64,64,128]{3,2,1,0:T(8,128)(2,1)} %weights_hbm.1, f32[16,4,512]{2,1,0:T(4,128)S(1)} %copy-done.7, bf16[512,1024]{1,0:T(8,128)(2,1)S(1)} %copy-done.1, bf16[512,1024]{1,0:T(8,128)(2,1)S(1)} %copy-done, ...), custom_call_target="tpu_custom_call" | custom-call | tf_op jit(solution)/shard_map/pallas_call | solution.py:289
  83.6 0.7 convert_bitcast_fusion
  84.4 3.1 %copy.14 = bf16[2,64,64,128]{3,2,1,0:T(8,128)(2,1)} copy(bf16[2,64,64,128]{3,2,1,0:T(8,128)(2,1)} %get-tuple-element.9) | data formatting | bytes 4194304
Async XLA Ops:
  0.6 1.2 %copy-start = (bf16[512,1024]{1,0:T(8,128)(2,1)S(1)}, bf16[512,1024]{1,0:T(8,128)(2,1)}, u32[]{:S(2)}) copy-start(bf16[512,1024]{1,0:T(8,128)(2,1)} %constant.17.clone.fine_l) | copy-start | bytes 3145732
  1.9 1.2 %copy-start.1 = (bf16[512,1024]{1,0:T(8,128)(2,1)S(1)}, bf16[512,1024]{1,0:T(8,128)(2,1)}, u32[]{:S(2)}) copy-start(bf16[512,1024]{1,0:T(8,128)(2,1)} %constant.16.clone.fine_h) | copy-start | bytes 3145732
  3.1 1.0 %copy-start.2 = (f32[16,8,1024]{2,1,0:T(8,128)S(1)}, f32[16,8,1024]{2,1,0:T(8,128)}, u32[]{:S(2)}) copy-start(f32[16,8,1024]{2,1,0:T(8,128)} %param.11) | copy-start | bytes 1572868
  4.1 1.0 %copy-start.3 = (bf16[512,512]{1,0:T(8,128)(2,1)S(1)}, bf16[512,512]{1,0:T(8,128)(2,1)}, u32[]{:S(2)}) copy-start(bf16[512,512]{1,0:T(8,128)(2,1)} %constant.23.clone.coarse_l) | copy-start | bytes 1572868
  5.2 1.0 %copy-start.4 = (bf16[512,512]{1,0:T(8,128)(2,1)S(1)}, bf16[512,512]{1,0:T(8,128)(2,1)}, u32[]{:S(2)}) copy-start(bf16[512,512]{1,0:T(8,128)(2,1)} %constant.22.clone.coarse_h) | copy-start | bytes 1572868
  6.2 1.0 %copy-start.5 = (bf16[512,512]{1,0:T(8,128)(2,1)S(1)}, bf16[512,512]{1,0:T(8,128)(2,1)}, u32[]{:S(2)}) copy-start(bf16[512,512]{1,0:T(8,128)(2,1)} %constant.21.clone.short_l) | copy-start | bytes 1572868
  7.3 1.0 %copy-start.6 = (bf16[512,512]{1,0:T(8,128)(2,1)S(1)}, bf16[512,512]{1,0:T(8,128)(2,1)}, u32[]{:S(2)}) copy-start(bf16[512,512]{1,0:T(8,128)(2,1)} %constant.20.clone.short_h) | copy-start | bytes 1572868
  8.3 0.9 %copy-start.7 = (f32[16,4,512]{2,1,0:T(4,128)S(1)}, f32[16,4,512]{2,1,0:T(4,128)}, u32[]{:S(2)}) copy-start(f32[16,4,512]{2,1,0:T(4,128)} %cot_hbm.1) | copy-start | bytes 393220
where the time goes:
time: 87.9 us; the launch traced here: 87.4 us
  Pallas kernels  74.4 us (85%)
  local copies, waits for them, and re-layouts  11.6 us (13%)
    pallas_call x1, Pallas kernels, local(): pl.pallas_call(kernel, out_shape=(jax.ShapeDtypeStruct((128, W), f32), ja...  74.4 us
    unnamed x17, local copies, waits for them, and re-layouts  11.6 us

commit v1 on v0

v1 whole, which is shorter than its diff:
```python
import math

import jax
import jax.numpy as jnp
import ml_dtypes
import numpy as np
from jax import lax
from jax.experimental import pallas as pl
from jax.experimental.pallas import tpu as pltpu
from jax.sharding import PartitionSpec as P

MESH = pl.DeviceIdType.MESH
ROWS = 128
CHANS = 4
KW = 256
KH = 256
W = 1024
H = 1024
GH = 512
GW = 512
HL = H // ROWS
TL = GH // ROWS
FAR_FIRST = sorted(
    ((dy, dx, dz) for dx in (2, 1, 3, 0) for dz in (2, 1, 3, 0) for dy in (4, 3, 5, 2, 6, 1, 7, 0) if (dy, dx, dz) != (0, 0, 0)),
    key=lambda o: -(min(o[0], 8 - o[0]) + min(o[1], 4 - o[1]) + 2 * min(o[2], 4 - o[2])),
)
NT = (((1,), (1,)), ((), ()))
NN = (((1,), (0,)), ((), ()))


def split_table(table):
    high = table.astype(np.float32).astype(ml_dtypes.bfloat16)
    low = (table - high.astype(np.float64)).astype(np.float32).astype(ml_dtypes.bfloat16)
    return high, low


def wave(first, second, length):
    angle = (first[:, None] * second[None, :]) % length * (2.0 * math.pi / length)
    return np.cos(angle), np.sin(angle)


def tables():
    dev = np.arange(ROWS)
    freq = np.arange(KH) - KH // 2
    fine, coarse = [], []
    for k in range(2):
        c, s = wave(2 * dev + k, np.arange(W // 2), W)
        fine += [c / math.sqrt(W), -s / math.sqrt(W)]
        c, s = wave(2 * dev + k, np.arange(GW // 2), GW)
        coarse += [c / math.sqrt(KH * KW), -s / math.sqrt(KH * KW)]
    c, s = wave(dev, dev, ROWS)
    ahead = np.block([[c, -s], [s, c]])
    back = np.concatenate([c, s], 1)
    out = []
    for table in (np.concatenate(fine, 0), np.concatenate(coarse, 0), ahead, back):
        out += split_table(table)
    twiddle = np.zeros((4, 8, KH))
    twiddle[0], twiddle[1] = (t / math.sqrt(H) for t in wave(np.arange(HL), freq, H))
    twiddle[2, :TL], twiddle[3, :TL] = wave(np.arange(TL), freq, GH)
    return out + [twiddle.astype(np.float32)]


def halves(value):
    high = value.astype(jnp.bfloat16)
    return high, (value - high.astype(jnp.float32)).astype(jnp.bfloat16)


def dot3(a, b, dims):
    def one(x, y):
        return lax.dot_general(x, y, dims, preferred_element_type=jnp.float32)

    return one(a[0], b[1]) + one(a[1], b[0]) + one(a[0], b[0])


def gelu_slope(values):
    cdf = 0.5 * (1.0 + lax.erf(values * (1.0 / math.sqrt(2.0))))
    pdf = jnp.exp(-0.5 * values * values) * (1.0 / math.sqrt(2.0 * math.pi))
    return cdf + values * pdf


def kernel(
    field_hbm, weights_hbm, cot_hbm, fine_h, fine_l, coarse_h, coarse_l, ahead_h, ahead_l, behind_h, behind_l, twiddle_hbm,
    left_h, left_l, t1h, t1l, gweights,
    field, weights, cot, t4h, t4l, wah, wal, wbh, wbl, twiddle,
    send1, recv1, send2, recv2, send3, recv3, send4, recv4,
    csend, crecv, mixed, part_r, part_i, back_r, back_i,
    in_sem, row_send, row_recv, chan_send, chan_recv,
):
    me = lax.axis_index("rows")
    mc = lax.axis_index("chan")
    me_y, me_x, me_z = me // 16, lax.rem(me // 4, 4), lax.rem(me, 4)
    others = [lax.rem(mc + k, CHANS) for k in range(1, CHANS)]

    def partner(offset):
        dy, dx, dz = offset
        return lax.rem(me_y + dy, 8) * 16 + lax.rem(me_x + dx, 4) * 4 + lax.rem(me_z + dz, 4)

    barrier = pltpu.get_barrier_semaphore()
    for offset in FAR_FIRST:
        pl.semaphore_signal(barrier, inc=1, device_id={"rows": partner(offset)}, device_id_type=MESH)
    for d in others:
        pl.semaphore_signal(barrier, inc=1, device_id={"chan": d}, device_id_type=MESH)

    loads = [
        pltpu.make_async_copy(src, dst, in_sem.at[n])
        for n, (src, dst) in enumerate(
            [
                (field_hbm, field), (fine_h, t1h), (fine_l, t1l), (ahead_h, wah), (ahead_l, wal), (twiddle_hbm, twiddle),
                (weights_hbm, weights), (behind_h, wbh), (behind_l, wbl), (coarse_h, t4h), (coarse_l, t4l), (cot_hbm, cot),
            ]
        )
    ]
    for load in loads:
        load.start()

    def spread_rows(send, recv, n):
        for offset in FAR_FIRST:
            d = partner(offset)
            pltpu.make_async_remote_copy(
                src_ref=send.at[d], dst_ref=recv.at[me], send_sem=row_send.at[n], recv_sem=row_recv.at[n],
                device_id={"rows": d}, device_id_type=MESH,
            ).start()
        recv[me] = send[me]

    def await_rows(recv, n):
        part = recv.at[pl.ds(0, ROWS - 1)]
        pltpu.make_async_copy(part, part, row_recv.at[n]).wait()

    def spread_chans(n):
        for d in others:
            pltpu.make_async_remote_copy(
                src_ref=csend.at[n, d], dst_ref=crecv.at[n, mc], send_sem=chan_send.at[n], recv_sem=chan_recv.at[n],
                device_id={"chan": d}, device_id_type=MESH,
            ).start()
        crecv[n, mc] = csend[n, mc]

    def await_chans(n):
        part = crecv.at[n, pl.ds(0, CHANS - 1)]
        pltpu.make_async_copy(part, part, chan_recv.at[n]).wait()

    def to_modes(rows, steps, table, n):
        product = dot3(halves(rows), (wah[...], wal[...]), NN)
        for k in range(2):
            for j in range(2):
                lanes = slice(128 * j, 128 * j + 128)
                real = imag = None
                for l in range(steps):
                    first = 16 * (steps * k + l)
                    re, im = product[first : first + 16, :128], product[first : first + 16, 128:]
                    c, s = twiddle[table, l : l + 1, lanes], twiddle[table + 1, l : l + 1, lanes]
                    more_r, more_i = c * re + s * im, c * im - s * re
                    real, imag = (more_r, more_i) if l == 0 else (real + more_r, imag + more_i)
                csend[n, 2 * k + j, 0:16, :] = real
                csend[n, 2 * k + j, 16:32, :] = imag
        spread_chans(n)

    def from_modes(n, steps, table):
        rows = []
        for l in range(steps):
            for k in range(2):
                real = imag = 0.0
                for j in range(2):
                    lanes = slice(128 * j, 128 * j + 128)
                    re, im = crecv[n, 2 * k + j, 0:16, :], crecv[n, 2 * k + j, 16:32, :]
                    c, s = twiddle[table, l : l + 1, lanes], twiddle[table + 1, l : l + 1, lanes]
                    real, imag = real + (c * re - s * im), imag + (s * re + c * im)
                rows.append(jnp.concatenate([real, -imag], axis=1))
                rows.append(jnp.concatenate([imag, real], axis=1))
        return dot3((wbh[...], wbl[...]), halves(jnp.concatenate(rows, axis=0)), NT)

    def give_modes(n, real, imag):
        for d in range(CHANS):
            csend[n, d, 0:16, :] = real[16 * d : 16 * d + 16, :]
            csend[n, d, 16:32, :] = imag[16 * d : 16 * d + 16, :]
        spread_chans(n)

    for n in (0, 1, 2):
        loads[n].wait()
    lines = jnp.concatenate([field[:, l, :] for l in range(HL)], axis=0)
    for k, folded in enumerate((lines[:, : W // 2] + lines[:, W // 2 :], lines[:, : W // 2] - lines[:, W // 2 :])):
        table = (t1h[256 * k : 256 * k + 256, :], t1l[256 * k : 256 * k + 256, :])
        spectra = dot3(table, halves(folded), NT)
        send1[:, 2 * k, :] = spectra[:128]
        send1[:, 2 * k + 1, :] = spectra[128:]
    pl.semaphore_wait(barrier, ROWS - 1 + CHANS - 1)
    spread_rows(send1, recv1, 0)
    for n in range(3, 12):
        loads[n].wait()
    await_rows(recv1, 0)

    rows = [jnp.concatenate([recv1[:, 2 * k, :].T, recv1[:, 2 * k + 1, :].T], axis=1) for k in range(2)]
    to_modes(jnp.concatenate(rows, axis=0), HL, 0, 0)

    def mix(ref, s, carry):
        def step(i, carry):
            out_r, out_i = carry
            xr, xi = ref[0, s, pl.ds(i, 1), :], ref[0, s, pl.ds(16 + i, 1), :]
            wr, wi = weights[0, 16 * s + i].astype(jnp.float32), weights[1, 16 * s + i].astype(jnp.float32)
            return out_r + (xr * wr - xi * wi), out_i + (xr * wi + xi * wr)

        return lax.fori_loop(0, 16, step, carry, unroll=4)

    zero = jnp.zeros((64, 128), jnp.float32)
    total = mix(csend, mc, (zero, zero))
    await_chans(0)
    for s in others:
        total = mix(crecv, s, total)
    give_modes(1, *total)
    await_chans(1)

    short = from_modes(1, TL, 2)
    for s in range(2):
        send2[:, s, :] = short[:, 128 * s : 128 * s + 128]
    spread_rows(send2, recv2, 1)
    await_rows(recv2, 1)
    turns = [recv2[:, s, :].T for s in range(2)]
    parts = []
    for k in range(2):
        rows = []
        for t in range(TL):
            first = 64 * (t % 2) + 32 * k
            rows.append(jnp.concatenate([turns[t // 2][first : first + 16], turns[t // 2][first + 16 : first + 32]], axis=1))
        table = (t4h[256 * k : 256 * k + 256, :], t4l[256 * k : 256 * k + 256, :])
        parts.append(dot3(halves(jnp.concatenate(rows, axis=0)), table, NN))
    values = jnp.concatenate([parts[0] + parts[1], parts[0] - parts[1]], axis=1)
    cotangent = jnp.concatenate([cot[:, t, :] for t in range(TL)], axis=0)
    grad_v = cotangent * gelu_slope(values)

    for k, folded in enumerate((grad_v[:, :256] + grad_v[:, 256:], grad_v[:, :256] - grad_v[:, 256:])):
        table = (t4h[256 * k : 256 * k + 256, :], t4l[256 * k : 256 * k + 256, :])
        cols = dot3(table, halves(folded), NT)
        send3[:, k, :] = jnp.concatenate([cols[:128], cols[128:]], axis=1)
    spread_rows(send3, recv3, 2)
    await_rows(recv3, 2)
    turns = [recv3[:, k, :].T for k in range(2)]
    rows = [jnp.concatenate([turn[:64], turn[64:]], axis=1) for turn in turns]
    to_modes(jnp.concatenate(rows, axis=0), TL, 2, 2)

    def terms(ref, s, i):
        gr, gi = ref[2, s, 0:16, :], ref[2, s, 16:32, :]
        own = pl.ds(pl.multiple_of(16 * s, 16), 16)
        wr, wi = weights[0, i, own, :].astype(jnp.float32), weights[1, i, own, :].astype(jnp.float32)
        real, imag = wr * gr + wi * gi, wr * gi - wi * gr
        return real[:8] + real[8:], imag[:8] + imag[8:]

    def unmix_own(i, _):
        part_r[i], part_i[i] = terms(csend, mc, i)
        return 0

    def unmix(i, _):
        real, imag = part_r[i], part_i[i]
        for s in others:
            more_r, more_i = terms(crecv, s, i)
            real, imag = real + more_r, imag + more_i
        back_r[pl.ds(i, 1), :] = jnp.sum(real, axis=0, keepdims=True)
        back_i[pl.ds(i, 1), :] = jnp.sum(imag, axis=0, keepdims=True)
        return 0

    lax.fori_loop(0, 64, unmix_own, 0, unroll=4)
    await_chans(2)
    lax.fori_loop(0, 64, unmix, 0, unroll=4)
    give_modes(3, back_r, back_i)
    await_chans(3)

    tall = from_modes(3, HL, 0)
    for s in range(4):
        send4[:, s, :] = tall[:, 128 * s : 128 * s + 128]
    spread_rows(send4, recv4, 3)

    def outer(i, _):
        s, c = i // 16, lax.rem(i, 16)
        xr, xi = crecv[0, s, pl.ds(c, 1), :], crecv[0, s, pl.ds(16 + c, 1), :]
        for o in range(CHANS):
            gr, gi = crecv[2, o, 0:16, :], crecv[2, o, 16:32, :]
            gweights[0, i, 16 * o : 16 * o + 16, :] = (xr * gr + xi * gi).astype(jnp.bfloat16)
            gweights[1, i, 16 * o : 16 * o + 16, :] = (xr * gi - xi * gr).astype(jnp.bfloat16)
        return 0

    lax.fori_loop(0, 64, outer, 0, unroll=4)
    for n, send in enumerate((send1, send2, send3)):
        part = send.at[pl.ds(0, ROWS - 1)]
        pltpu.make_async_copy(part, part, row_send.at[n]).wait()
    for n in range(4):
        part = csend.at[n, pl.ds(0, CHANS - 1)]
        pltpu.make_async_copy(part, part, chan_send.at[n]).wait()
    await_rows(recv4, 3)
    for s in range(4):
        turn = recv4[:, s, :].T
        for l in range(2):
            for u in range(4):
                mixed[u, pl.ds(2 * s + l, 16, stride=HL), :] = turn[64 * l + 16 * u : 64 * l + 16 * u + 16]
    for k in range(2):
        high, low = halves(jnp.concatenate([mixed[2 * k], mixed[2 * k + 1]], axis=1))
        left_h[128 * k : 128 * k + 128, :] = high
        left_l[128 * k : 128 * k + 128, :] = low
    part = send4.at[pl.ds(0, ROWS - 1)]
    pltpu.make_async_copy(part, part, row_send.at[3]).wait()


def finish(left_h, left_l, t1h, t1l, gweights, gfield, gweights_hbm, sem):
    store = pltpu.make_async_copy(gweights, gweights_hbm, sem)
    store.start()
    parts = []
    for k in range(2):
        lines, table = slice(128 * k, 128 * k + 128), slice(256 * k, 256 * k + 256)
        parts.append(dot3((left_h[lines, :], left_l[lines, :]), (t1h[table, :], t1l[table, :]), NN))
    whole = jnp.concatenate([parts[0] + parts[1], parts[0] - parts[1]], axis=1)
    gfield[...] = whole.reshape(gfield.shape).astype(jnp.bfloat16)
    store.wait()


def local(field, weights, cotangent):
    f32, bf16 = jnp.float32, jnp.bfloat16
    consts = [jnp.asarray(t) for t in tables()]
    anywhere = pl.BlockSpec(memory_space=pl.ANY)
    inside = pl.BlockSpec(memory_space=pltpu.VMEM)
    operands = [pltpu.with_memory_space_constraint(x, pltpu.HBM) for x in (field, weights, cotangent, *consts)]
    kept = pl.pallas_call(
        kernel,
        out_shape=(
            pltpu.VMEM((256, 256), bf16),
            pltpu.VMEM((256, 256), bf16),
            pltpu.VMEM(consts[0].shape, bf16),
            pltpu.VMEM(consts[1].shape, bf16),
            pltpu.VMEM(weights.shape, bf16),
        ),
        in_specs=[anywhere] * len(operands),
        out_specs=(inside,) * 5,
        scratch_shapes=[
            pltpu.VMEM(field.shape, f32),
            pltpu.VMEM(weights.shape, bf16),
            pltpu.VMEM(cotangent.shape, f32),
            *[pltpu.VMEM(t.shape, t.dtype) for t in consts[2:]],
            *[pltpu.VMEM((ROWS, n, 128), f32) for n in (4, 4, 2, 2, 2, 2, 4, 4)],
            pltpu.VMEM((4, CHANS, 32, 128), f32),
            pltpu.VMEM((4, CHANS, 32, 128), f32),
            pltpu.VMEM((4, 128, 128), f32),
            *[pltpu.VMEM((64, 8, 128), f32)] * 2,
            *[pltpu.VMEM((64, 128), f32)] * 2,
            pltpu.SemaphoreType.DMA((12,)),
            pltpu.SemaphoreType.DMA((4,)),
            pltpu.SemaphoreType.DMA((4,)),
            pltpu.SemaphoreType.DMA((4,)),
            pltpu.SemaphoreType.DMA((4,)),
        ],
        compiler_params=pltpu.CompilerParams(
            collective_id=0, has_side_effects=True, vmem_limit_bytes=40 * 2**20
        ),
    )(*operands)
    return pl.pallas_call(
        finish,
        out_shape=(
            jax.ShapeDtypeStruct(field.shape, bf16),
            jax.ShapeDtypeStruct(weights.shape, bf16),
        ),
        in_specs=[inside] * 5,
        out_specs=(inside, anywhere),
        scratch_shapes=[pltpu.SemaphoreType.DMA],
        compiler_params=pltpu.CompilerParams(vmem_limit_bytes=16 * 2**20),
    )(*kept)


def solution(mesh):
    spread = P("chan", "rows", None)
    by_mode = P(None, None, None, ("rows", "chan"))
    return jax.shard_map(
        local, mesh=mesh, in_specs=(spread, by_mode, spread), out_specs=(spread, by_mode), check_vma=False
    )
```

time: 87.9 us -> 72.5 us (0.82)
  local copies, waits for them, and re-layouts: 11.6 us -> 0 us
  Pallas kernels: 74.4 us -> 71.8 us
    unnamed x17 -> x0, local copies, waits for them, and re-layouts: 11.6 us -> none
    pallas_call x1 -> x2, Pallas kernels: 74.4 us -> 71.8 us  [the longest x1 69.6 us: local(): pl.pallas_call(kernel, out_shape=(pltpu.VMEM((256, 256), bf16), pltpu.VME...]
where the time goes in v1:
time: 72.5 us; the launch traced here: 72.4 us
  Pallas kernels  71.8 us (99%)
    pallas_call x1, Pallas kernels, local(): pl.pallas_call(kernel, out_shape=(pltpu.VMEM((256, 256), bf16), pltpu.VME...  69.6 us
    pallas_call x1, Pallas kernels, local(): pl.pallas_call(finish, out_shape=(jax.ShapeDtypeStruct(field.shape, bf16)...  2.17 us

profile of v1, /device:TPU:1, one launch (start us, length us, event | category | flops | bytes accessed | tf_op | source)
XLA Modules:
  0.0 72.4 jit_solution(2342885470295609910)
XLA Ops:
  0.6 69.6 %shard_map.131 = (bf16[256,256]{1,0:T(8,128)(2,1)S(1)}, bf16[256,256]{1,0:T(8,128)(2,1)S(1)}, bf16[512,512]{1,0:T(8,128)(2,1)S(1)}, bf16[512,512]{1,0:T(8,128)(2,1)S(1)}, bf16[2,64,64,128]{3,2,1,0:T(8,128)(2,1)S(1)}) custom-call(f32[16,8,1024]{2,1,0:T(8,128)} %field_hbm.1, bf16[2,64,64,128]{3,2,1,0:T(8,128)(2,1)} %weights_hbm.1, f32[16,4,512]{2,1,0:T(4,128)} %cot_hbm.1, ...), custom_call_target="tpu_custom_call" | custom-call | tf_op jit(solution)/shard_map/pallas_call | solution.py:318
  70.2 2.2 %shard_map.132 = (bf16[16,8,1024]{2,1,0:T(8,128)(2,1)}, bf16[2,64,64,128]{3,2,1,0:T(8,128)(2,1)}) custom-call(bf16[256,256]{1,0:T(8,128)(2,1)S(1)} %get-tuple-element.7.left_h, bf16[256,256]{1,0:T(8,128)(2,1)S(1)} %get-tuple-element.8.left_l, bf16[512,512]{1,0:T(8,128)(2,1)S(1)} %get-tuple-element.9.t1h, bf16[512,512]{1,0:T(8,128)(2,1)S(1)} %get-tuple-element.10.t1l, ...), custom_call_target="tpu_custom_call" | custom-call | tf_op jit(solution)/shard_map/pallas_call | solution.py:350

commit v2 on v1

v2 whole, which is shorter than its diff:
```python
import math

import jax
import jax.numpy as jnp
import ml_dtypes
import numpy as np
from jax import lax
from jax.experimental import pallas as pl
from jax.experimental.pallas import tpu as pltpu
from jax.sharding import PartitionSpec as P

MESH = pl.DeviceIdType.MESH
ROWS = 128
CHANS = 4
KW = 256
KH = 256
W = 1024
H = 1024
GH = 512
GW = 512
HL = H // ROWS
TL = GH // ROWS
EIGHT = (4, 3, 5, 2, 6, 1, 7, 0)
FAR_FIRST = sorted(
    ((dy, dx, dz) for dx in (2, 1, 3, 0) for dz in EIGHT for dy in EIGHT if (dy, dx, dz) != (0, 0, 0)),
    key=lambda o: -(min(o[0], 8 - o[0]) + min(o[1], 4 - o[1]) + min(o[2], 8 - o[2])),
)
NT = (((1,), (1,)), ((), ()))
NN = (((1,), (0,)), ((), ()))


def split_table(table):
    high = table.astype(np.float32).astype(ml_dtypes.bfloat16)
    low = (table - high.astype(np.float64)).astype(np.float32).astype(ml_dtypes.bfloat16)
    return high, low


def wave(first, second, length):
    angle = (first[:, None] * second[None, :]) % length * (2.0 * math.pi / length)
    return np.cos(angle), np.sin(angle)


def tables():
    dev = np.arange(ROWS)
    freq = np.arange(KH) - KH // 2
    fine, coarse = [], []
    for k in range(2):
        c, s = wave(2 * dev + k, np.arange(W // 2), W)
        fine += [c / math.sqrt(W), -s / math.sqrt(W)]
        c, s = wave(2 * dev + k, np.arange(GW // 2), GW)
        coarse += [c / math.sqrt(KH * KW), -s / math.sqrt(KH * KW)]
    c, s = wave(dev, dev, ROWS)
    ahead = np.block([[c, -s], [s, c]])
    back = np.concatenate([c, s], 1)
    out = []
    for table in (np.concatenate(fine, 0), np.concatenate(coarse, 0), ahead, back):
        out += split_table(table)
    twiddle = np.zeros((4, 8, KH))
    twiddle[0], twiddle[1] = (t / math.sqrt(H) for t in wave(np.arange(HL), freq, H))
    twiddle[2, :TL], twiddle[3, :TL] = wave(np.arange(TL), freq, GH)
    return out + [twiddle.astype(np.float32)]


def halves(value):
    high = value.astype(jnp.bfloat16)
    return high, (value - high.astype(jnp.float32)).astype(jnp.bfloat16)


def dot3(a, b, dims):
    def one(x, y):
        return lax.dot_general(x, y, dims, preferred_element_type=jnp.float32)

    return one(a[0], b[1]) + one(a[1], b[0]) + one(a[0], b[0])


def gelu_slope(values):
    cdf = 0.5 * (1.0 + lax.erf(values * (1.0 / math.sqrt(2.0))))
    pdf = jnp.exp(-0.5 * values * values) * (1.0 / math.sqrt(2.0 * math.pi))
    return cdf + values * pdf


def kernel(
    field_hbm, weights_hbm, cot_hbm, fine_h, fine_l, coarse_h, coarse_l, ahead_h, ahead_l, behind_h, behind_l, twiddle_hbm,
    left_h, left_l, t1h, t1l, gweights,
    field, weights, cot, t4h, t4l, wah, wal, wbh, wbl, twiddle,
    send1, recv1, send2, recv2, send3, recv3, send4, recv4,
    csend, crecv, mixed, part_r, part_i, back_r, back_i,
    in_sem, row_send, row_recv, chan_send, chan_recv,
):
    me = lax.axis_index("rows")
    mc = lax.axis_index("chan")
    core, low = lax.rem(mc, 2), mc // 2
    me_y, me_x, me_z = me // 16, lax.rem(me // 4, 4), 2 * lax.rem(me, 4) + low
    mate = {"chan": mc + 1 - 2 * core}

    def partner(offset):
        dy, dx, dz = offset
        z = lax.rem(me_z + dz, 8)
        return lax.rem(me_y + dy, 8) * 16 + lax.rem(me_x + dx, 4) * 4 + z // 2, lax.rem(z, 2)

    barrier = pltpu.get_barrier_semaphore()
    for offset in FAR_FIRST:
        r, z = partner(offset)
        pl.semaphore_signal(barrier, inc=1, device_id={"rows": r, "chan": 2 * z + core}, device_id_type=MESH)
    pl.semaphore_signal(barrier, inc=1, device_id=mate, device_id_type=MESH)

    loads = [
        pltpu.make_async_copy(src, dst, in_sem.at[n])
        for n, (src, dst) in enumerate(
            [
                (field_hbm, field), (fine_h, t1h), (fine_l, t1l), (ahead_h, wah), (ahead_l, wal), (twiddle_hbm, twiddle),
                (weights_hbm, weights), (behind_h, wbh), (behind_l, wbl), (coarse_h, t4h), (coarse_l, t4l), (cot_hbm, cot),
            ]
        )
    ]
    for load in loads:
        load.start()

    def spread_rows(send, recv, n):
        def copy(r, z, device, which):
            pltpu.make_async_remote_copy(
                src_ref=send.at[r, z], dst_ref=recv.at[me, low], send_sem=row_send.at[n, which],
                recv_sem=row_recv.at[n, which], device_id=device, device_id_type=MESH,
            ).start()

        same = lax.rem(low + 1, 2)
        for dy, dx, dz in FAR_FIRST:
            r, z = partner((dy, dx, dz))
            if (dy, dx) == (0, 0) and dz in (1, 7):
                continue
            copy(r, z, {"rows": r, "chan": 2 * z + core}, 0)
        other = lax.rem(me_z + 7 + 2 * low, 8)
        r, z = me // 4 * 4 + other // 2, lax.rem(other, 2)
        copy(r, z, {"rows": r, "chan": 2 * z + core}, 0)
        copy(me, same, {"chan": 2 * same + core}, 1)
        recv[me, low] = send[me, low]

    def all_but_one(ref):
        return ref.at[pl.ds(0, ROWS - 1)]

    def await_rows(recv, n):
        part = all_but_one(recv)
        pltpu.make_async_copy(part, part, row_recv.at[n, 0]).wait()
        part = recv.at[me, lax.rem(low + 1, 2)]
        pltpu.make_async_copy(part, part, row_recv.at[n, 1]).wait()

    def await_sent(send, n):
        part = all_but_one(send)
        pltpu.make_async_copy(part, part, row_send.at[n, 0]).wait()
        part = send.at[me, lax.rem(low + 1, 2)]
        pltpu.make_async_copy(part, part, row_send.at[n, 1]).wait()

    def swap(n):
        return pltpu.make_async_remote_copy(
            src_ref=csend.at[n, 1 - core], dst_ref=crecv.at[n, core], send_sem=chan_send.at[n], recv_sem=chan_recv.at[n],
            device_id=mate, device_id_type=MESH,
        )

    def start_swap(n):
        swap(n).start()
        crecv[n, core] = csend[n, core]

    def to_modes(rows, steps, table, n):
        product = dot3(halves(rows), (wah[...], wal[...]), NN)
        for z in range(2):
            for j in range(2):
                lanes = slice(128 * j, 128 * j + 128)
                real = imag = None
                for l in range(steps):
                    first = 16 * (steps * z + l)
                    re, im = product[first : first + 16, :128], product[first : first + 16, 128:]
                    c, s = twiddle[table, l : l + 1, lanes], twiddle[table + 1, l : l + 1, lanes]
                    more_r, more_i = c * re + s * im, c * im - s * re
                    real, imag = (more_r, more_i) if l == 0 else (real + more_r, imag + more_i)
                csend[n, j, z, 0:16, :] = real
                csend[n, j, z, 16:32, :] = imag
        start_swap(n)

    def from_modes(n, steps, table):
        rows = []
        for z in range(2):
            for l in range(steps):
                real = imag = 0.0
                for j in range(2):
                    lanes = slice(128 * j, 128 * j + 128)
                    re, im = crecv[n, j, z, 0:16, :], crecv[n, j, z, 16:32, :]
                    c, s = twiddle[table, l : l + 1, lanes], twiddle[table + 1, l : l + 1, lanes]
                    real, imag = real + (c * re - s * im), imag + (s * re + c * im)
                rows.append(jnp.concatenate([real, -imag], axis=1))
                rows.append(jnp.concatenate([imag, real], axis=1))
        return dot3((wbh[...], wbl[...]), halves(jnp.concatenate(rows, axis=0)), NT)

    def give_modes(n, real, imag):
        for z in range(2):
            for c in range(2):
                first = 16 * (2 * z + c)
                csend[n, c, z, 0:16, :] = real[first : first + 16, :]
                csend[n, c, z, 16:32, :] = imag[first : first + 16, :]
        start_swap(n)

    for n in (0, 1, 2):
        loads[n].wait()
    lines = jnp.concatenate([field[:, l, :] for l in range(HL)], axis=0)
    for k, folded in enumerate((lines[:, : W // 2] + lines[:, W // 2 :], lines[:, : W // 2] - lines[:, W // 2 :])):
        table = (t1h[256 * k : 256 * k + 256, :], t1l[256 * k : 256 * k + 256, :])
        spectra = dot3(table, halves(folded), NT)
        send1[:, k, 0, :] = spectra[:128]
        send1[:, k, 1, :] = spectra[128:]
    pl.semaphore_wait(barrier, 2 * ROWS)
    spread_rows(send1, recv1, 0)
    for n in range(3, 12):
        loads[n].wait()
    await_rows(recv1, 0)

    rows = [jnp.concatenate([recv1[:, z, 0, :].T, recv1[:, z, 1, :].T], axis=1) for z in range(2)]
    to_modes(jnp.concatenate(rows, axis=0), HL, 0, 0)

    def mix(ref, origin, z, carry):
        def step(i, carry):
            out_r, out_i = carry
            xr, xi = ref[0, origin, z, pl.ds(i, 1), :], ref[0, origin, z, pl.ds(16 + i, 1), :]
            channel = 32 * z + 16 * origin + i
            wr, wi = weights[0, channel].astype(jnp.float32), weights[1, channel].astype(jnp.float32)
            return out_r + (xr * wr - xi * wi), out_i + (xr * wi + xi * wr)

        return lax.fori_loop(0, 16, step, carry, unroll=4)

    zero = jnp.zeros((64, 128), jnp.float32)
    total = (zero, zero)
    for z in range(2):
        total = mix(csend, core, z, total)
    swap(0).wait_recv()
    for z in range(2):
        total = mix(crecv, 1 - core, z, total)
    give_modes(1, *total)
    swap(1).wait_recv()

    short = from_modes(1, TL, 2)
    for s in range(2):
        send2[:, s, 0, :] = short[:, 128 * s : 128 * s + 128]
    spread_rows(send2, recv2, 1)
    await_rows(recv2, 1)
    turns = [recv2[:, k, 0, :].T for k in range(2)]
    parts = []
    for k in range(2):
        rows = []
        for t in range(TL):
            rows.append(jnp.concatenate([turns[k][32 * t : 32 * t + 16], turns[k][32 * t + 16 : 32 * t + 32]], axis=1))
        table = (t4h[256 * k : 256 * k + 256, :], t4l[256 * k : 256 * k + 256, :])
        parts.append(dot3(halves(jnp.concatenate(rows, axis=0)), table, NN))
    values = jnp.concatenate([parts[0] + parts[1], parts[0] - parts[1]], axis=1)
    cotangent = jnp.concatenate([cot[:, t, :] for t in range(TL)], axis=0)
    grad_v = cotangent * gelu_slope(values)

    for k, folded in enumerate((grad_v[:, :256] + grad_v[:, 256:], grad_v[:, :256] - grad_v[:, 256:])):
        table = (t4h[256 * k : 256 * k + 256, :], t4l[256 * k : 256 * k + 256, :])
        cols = dot3(table, halves(folded), NT)
        send3[:, k, 0, :] = jnp.concatenate([cols[:128], cols[128:]], axis=1)
    spread_rows(send3, recv3, 2)
    await_rows(recv3, 2)
    turns = [recv3[:, z, 0, :].T for z in range(2)]
    rows = [jnp.concatenate([turn[:64], turn[64:]], axis=1) for turn in turns]
    to_modes(jnp.concatenate(rows, axis=0), TL, 2, 2)

    def terms(ref, origin, i):
        real = imag = 0.0
        for z in range(2):
            gr, gi = ref[2, origin, z, 0:16, :], ref[2, origin, z, 16:32, :]
            own = pl.ds(pl.multiple_of(32 * z + 16 * origin, 16), 16)
            wr, wi = weights[0, i, own, :].astype(jnp.float32), weights[1, i, own, :].astype(jnp.float32)
            real, imag = real + (wr * gr + wi * gi), imag + (wr * gi - wi * gr)
        return real[:8] + real[8:], imag[:8] + imag[8:]

    def unmix_own(i, _):
        part_r[i], part_i[i] = terms(csend, core, i)
        return 0

    def unmix(i, _):
        real, imag = terms(crecv, 1 - core, i)
        back_r[pl.ds(i, 1), :] = jnp.sum(part_r[i] + real, axis=0, keepdims=True)
        back_i[pl.ds(i, 1), :] = jnp.sum(part_i[i] + imag, axis=0, keepdims=True)
        return 0

    lax.fori_loop(0, 64, unmix_own, 0, unroll=4)
    swap(2).wait_recv()
    lax.fori_loop(0, 64, unmix, 0, unroll=4)
    give_modes(3, back_r, back_i)
    swap(3).wait_recv()

    tall = from_modes(3, HL, 0)
    for s in range(4):
        send4[:, s // 2, s % 2, :] = tall[:, 128 * s : 128 * s + 128]
    spread_rows(send4, recv4, 3)

    def outer(i, _):
        z, origin, c = i // 32, lax.rem(i // 16, 2), lax.rem(i, 16)
        xr, xi = crecv[0, origin, z, pl.ds(c, 1), :], crecv[0, origin, z, pl.ds(16 + c, 1), :]
        for o in range(CHANS):
            gr, gi = crecv[2, o % 2, o // 2, 0:16, :], crecv[2, o % 2, o // 2, 16:32, :]
            gweights[0, i, 16 * o : 16 * o + 16, :] = (xr * gr + xi * gi).astype(jnp.bfloat16)
            gweights[1, i, 16 * o : 16 * o + 16, :] = (xr * gi - xi * gr).astype(jnp.bfloat16)
        return 0

    lax.fori_loop(0, 64, outer, 0, unroll=4)
    for n, send in enumerate((send1, send2, send3)):
        await_sent(send, n)
    for n in range(4):
        swap(n).wait_send()
    await_rows(recv4, 3)
    for k in range(2):
        for s in range(2):
            turn = recv4[:, k, s, :].T
            for l in range(4):
                for p in range(2):
                    first = 32 * l + 16 * p
                    mixed[2 * k + p, pl.ds(4 * s + l, 16, stride=HL), :] = turn[first : first + 16]
    for k in range(2):
        high, low_half = halves(jnp.concatenate([mixed[2 * k], mixed[2 * k + 1]], axis=1))
        left_h[128 * k : 128 * k + 128, :] = high
        left_l[128 * k : 128 * k + 128, :] = low_half
    await_sent(send4, 3)


def finish(left_h, left_l, t1h, t1l, gweights, gfield, gweights_hbm, sem):
    stores = []
    for n in range(8):
        part = (n // 4, pl.ds(n % 4 * 16, 16))
        stores.append(pltpu.make_async_copy(gweights.at[part], gweights_hbm.at[part], sem.at[n]))
        stores[-1].start()
    parts = []
    for k in range(2):
        lines, table = slice(128 * k, 128 * k + 128), slice(256 * k, 256 * k + 256)
        parts.append(dot3((left_h[lines, :], left_l[lines, :]), (t1h[table, :], t1l[table, :]), NN))
    whole = jnp.concatenate([parts[0] + parts[1], parts[0] - parts[1]], axis=1)
    gfield[...] = whole.reshape(gfield.shape).astype(jnp.bfloat16)
    for store in stores:
        store.wait()


def local(field, weights, cotangent):
    f32, bf16 = jnp.float32, jnp.bfloat16
    consts = [jnp.asarray(t) for t in tables()]
    anywhere = pl.BlockSpec(memory_space=pl.ANY)
    inside = pl.BlockSpec(memory_space=pltpu.VMEM)
    operands = [pltpu.with_memory_space_constraint(x, pltpu.HBM) for x in (field, weights, cotangent, *consts)]
    kept = pl.pallas_call(
        kernel,
        out_shape=(
            pltpu.VMEM((256, 256), bf16),
            pltpu.VMEM((256, 256), bf16),
            pltpu.VMEM(consts[0].shape, bf16),
            pltpu.VMEM(consts[1].shape, bf16),
            pltpu.VMEM(weights.shape, bf16),
        ),
        in_specs=[anywhere] * len(operands),
        out_specs=(inside,) * 5,
        scratch_shapes=[
            pltpu.VMEM(field.shape, f32),
            pltpu.VMEM(weights.shape, bf16),
            pltpu.VMEM(cotangent.shape, f32),
            *[pltpu.VMEM(t.shape, t.dtype) for t in consts[2:]],
            *[pltpu.VMEM((ROWS, 2, n, 128), f32) for n in (2, 2, 1, 1, 1, 1, 2, 2)],
            pltpu.VMEM((4, 2, 2, 32, 128), f32),
            pltpu.VMEM((4, 2, 2, 32, 128), f32),
            pltpu.VMEM((4, 128, 128), f32),
            *[pltpu.VMEM((64, 8, 128), f32)] * 2,
            *[pltpu.VMEM((64, 128), f32)] * 2,
            pltpu.SemaphoreType.DMA((12,)),
            pltpu.SemaphoreType.DMA((4, 2)),
            pltpu.SemaphoreType.DMA((4, 2)),
            pltpu.SemaphoreType.DMA((4,)),
            pltpu.SemaphoreType.DMA((4,)),
        ],
        compiler_params=pltpu.CompilerParams(
            collective_id=0, has_side_effects=True, vmem_limit_bytes=40 * 2**20
        ),
    )(*operands)
    return pl.pallas_call(
        finish,
        out_shape=(
            jax.ShapeDtypeStruct(field.shape, bf16),
            jax.ShapeDtypeStruct(weights.shape, bf16),
        ),
        in_specs=[inside] * 5,
        out_specs=(inside, anywhere),
        scratch_shapes=[pltpu.SemaphoreType.DMA((8,))],
        compiler_params=pltpu.CompilerParams(vmem_limit_bytes=16 * 2**20),
    )(*kept)


def solution(mesh):
    spread = P("chan", "rows", None)
    by_mode = P(None, None, None, ("rows", "chan"))
    return jax.shard_map(
        local, mesh=mesh, in_specs=(spread, by_mode, spread), out_specs=(spread, by_mode), check_vma=False
    )
```

time: 72.5 us -> 66 us (0.910)
  Pallas kernels: 71.8 us -> 64.9 us
    pallas_call x1, Pallas kernels: 69.6 us -> 62.7 us  [local(): pl.pallas_call(kernel, out_shape=(pltpu.VMEM((256, 256), bf16), pltpu.VME...]
where the time goes in v2:
time: 66 us; the launch traced here: 65.5 us
  Pallas kernels  64.9 us (98%)
    pallas_call x1, Pallas kernels, local(): pl.pallas_call(kernel, out_shape=(pltpu.VMEM((256, 256), bf16), pltpu.VME...  62.7 us
    pallas_call x1, Pallas kernels, local(): pl.pallas_call(finish, out_shape=(jax.ShapeDtypeStruct(field.shape, bf16)...  2.22 us

profile of v2, /device:TPU:1, one launch (start us, length us, event | category | flops | bytes accessed | tf_op | source)
XLA Modules:
  0.0 65.5 jit_solution(17441337952891119295)
XLA Ops:
  0.6 62.7 %shard_map.131 = (bf16[256,256]{1,0:T(8,128)(2,1)S(1)}, bf16[256,256]{1,0:T(8,128)(2,1)S(1)}, bf16[512,512]{1,0:T(8,128)(2,1)S(1)}, bf16[512,512]{1,0:T(8,128)(2,1)S(1)}, bf16[2,64,64,128]{3,2,1,0:T(8,128)(2,1)S(1)}) custom-call(f32[16,8,1024]{2,1,0:T(8,128)} %field_hbm.1, bf16[2,64,64,128]{3,2,1,0:T(8,128)(2,1)} %weights_hbm.1, f32[16,4,512]{2,1,0:T(4,128)} %cot_hbm.1, ...), custom_call_target="tpu_custom_call" | custom-call | tf_op jit(solution)/shard_map/pallas_call | solution.py:346
  63.3 2.2 %shard_map.132 = (bf16[16,8,1024]{2,1,0:T(8,128)(2,1)}, bf16[2,64,64,128]{3,2,1,0:T(8,128)(2,1)}) custom-call(bf16[256,256]{1,0:T(8,128)(2,1)S(1)} %get-tuple-element.7.left_h, bf16[256,256]{1,0:T(8,128)(2,1)S(1)} %get-tuple-element.8.left_l, bf16[512,512]{1,0:T(8,128)(2,1)S(1)} %get-tuple-element.9.t1h, bf16[512,512]{1,0:T(8,128)(2,1)S(1)} %get-tuple-element.10.t1l, ...), custom_call_target="tpu_custom_call" | custom-call | tf_op jit(solution)/shard_map/pallas_call | solution.py:378

commit v3 on v2

--- a/solution.py
+++ b/solution.py
@@ -93,15 +93,14 @@
     me_y, me_x, me_z = me // 16, lax.rem(me // 4, 4), 2 * lax.rem(me, 4) + low
     mate = {"chan": mc + 1 - 2 * core}
 
-    def partner(offset):
-        dy, dx, dz = offset
-        z = lax.rem(me_z + dz, 8)
-        return lax.rem(me_y + dy, 8) * 16 + lax.rem(me_x + dx, 4) * 4 + z // 2, lax.rem(z, 2)
+    at_yx = [[lax.rem(me_y + dy, 8) * 32 + lax.rem(me_x + dx, 4) * 8 for dx in range(4)] for dy in range(8)]
+    at_z = [lax.rem(me_z + dz, 8) for dz in range(8)]
+    own = 2 * me + low
+    partners = [at_yx[dy][dx] + at_z[dz] for dy, dx, dz in FAR_FIRST]
 
     barrier = pltpu.get_barrier_semaphore()
-    for offset in FAR_FIRST:
-        r, z = partner(offset)
-        pl.semaphore_signal(barrier, inc=1, device_id={"rows": r, "chan": 2 * z + core}, device_id_type=MESH)
+    for d in partners:
+        pl.semaphore_signal(barrier, inc=1, device_id=2 * d + core, device_id_type=pl.DeviceIdType.LOGICAL)
     pl.semaphore_signal(barrier, inc=1, device_id=mate, device_id_type=MESH)
 
     loads = [
@@ -117,38 +116,27 @@
         load.start()
 
     def spread_rows(send, recv, n):
-        def copy(r, z, device, which):
+        source, target = flat(send), flat(recv)
+        for d in partners:
             pltpu.make_async_remote_copy(
-                src_ref=send.at[r, z], dst_ref=recv.at[me, low], send_sem=row_send.at[n, which],
-                recv_sem=row_recv.at[n, which], device_id=device, device_id_type=MESH,
+                src_ref=source.at[d], dst_ref=target.at[own], send_sem=row_send.at[n], recv_sem=row_recv.at[n],
+                device_id=2 * d + core, device_id_type=pl.DeviceIdType.LOGICAL,
             ).start()
-
-        same = lax.rem(low + 1, 2)
-        for dy, dx, dz in FAR_FIRST:
-            r, z = partner((dy, dx, dz))
-            if (dy, dx) == (0, 0) and dz in (1, 7):
-                continue
-            copy(r, z, {"rows": r, "chan": 2 * z + core}, 0)
-        other = lax.rem(me_z + 7 + 2 * low, 8)
-        r, z = me // 4 * 4 + other // 2, lax.rem(other, 2)
-        copy(r, z, {"rows": r, "chan": 2 * z + core}, 0)
-        copy(me, same, {"chan": 2 * same + core}, 1)
         recv[me, low] = send[me, low]
 
+    def flat(ref):
+        return ref.reshape(2 * ROWS, *ref.shape[2:])
+
     def all_but_one(ref):
-        return ref.at[pl.ds(0, ROWS - 1)]
+        return flat(ref).at[pl.ds(0, 2 * ROWS - 1)]
 
     def await_rows(recv, n):
         part = all_but_one(recv)
-        pltpu.make_async_copy(part, part, row_recv.at[n, 0]).wait()
-        part = recv.at[me, lax.rem(low + 1, 2)]
-        pltpu.make_async_copy(part, part, row_recv.at[n, 1]).wait()
+        pltpu.make_async_copy(part, part, row_recv.at[n]).wait()
 
     def await_sent(send, n):
         part = all_but_one(send)
-        pltpu.make_async_copy(part, part, row_send.at[n, 0]).wait()
-        part = send.at[me, lax.rem(low + 1, 2)]
-        pltpu.make_async_copy(part, part, row_send.at[n, 1]).wait()
+        pltpu.make_async_copy(part, part, row_send.at[n]).wait()
 
     def swap(n):
         return pltpu.make_async_remote_copy(
@@ -321,7 +309,7 @@
     await_sent(send4, 3)
 
 
-def finish(left_h, left_l, t1h, t1l, gweights, gfield, gweights_hbm, sem):
+def finish(left_h, left_l, t1h, t1l, gweights, gfield_hbm, gweights_hbm, gfield, sem):
     stores = []
     for n in range(8):
         part = (n // 4, pl.ds(n % 4 * 16, 16))
@@ -333,6 +321,8 @@
         parts.append(dot3((left_h[lines, :], left_l[lines, :]), (t1h[table, :], t1l[table, :]), NN))
     whole = jnp.concatenate([parts[0] + parts[1], parts[0] - parts[1]], axis=1)
     gfield[...] = whole.reshape(gfield.shape).astype(jnp.bfloat16)
+    stores.append(pltpu.make_async_copy(gfield, gfield_hbm, sem.at[8]))
+    stores[-1].start()
     for store in stores:
         store.wait()
 
@@ -366,8 +356,8 @@
             *[pltpu.VMEM((64, 8, 128), f32)] * 2,
             *[pltpu.VMEM((64, 128), f32)] * 2,
             pltpu.SemaphoreType.DMA((12,)),
-            pltpu.SemaphoreType.DMA((4, 2)),
-            pltpu.SemaphoreType.DMA((4, 2)),
+            pltpu.SemaphoreType.DMA((4,)),
+            pltpu.SemaphoreType.DMA((4,)),
             pltpu.SemaphoreType.DMA((4,)),
             pltpu.SemaphoreType.DMA((4,)),
         ],
@@ -382,8 +372,8 @@
             jax.ShapeDtypeStruct(weights.shape, bf16),
         ),
         in_specs=[inside] * 5,
-        out_specs=(inside, anywhere),
-        scratch_shapes=[pltpu.SemaphoreType.DMA((8,))],
+        out_specs=(anywhere, anywhere),
+        scratch_shapes=[pltpu.VMEM(field.shape, bf16), pltpu.SemaphoreType.DMA((9,))],
         compiler_params=pltpu.CompilerParams(vmem_limit_bytes=16 * 2**20),
     )(*kept)
 

time: 66 us -> 65.4 us (level)
    pallas_call x1, Pallas kernels: 2.22 us -> 1.48 us  [local(): pl.pallas_call(finish, out_shape=(jax.ShapeDtypeStruct(field.shape, bf16)...]
where the time goes in v3:
time: 65.4 us; the launch traced here: 65 us
  Pallas kernels  64.4 us (98%)
    pallas_call x1, Pallas kernels, local(): pl.pallas_call(kernel, out_shape=(pltpu.VMEM((256, 256), bf16), pltpu.VME...  62.9 us
    pallas_call x1, Pallas kernels, local(): pl.pallas_call(finish, out_shape=(jax.ShapeDtypeStruct(field.shape, bf16)...  1.48 us

profile of v3, /device:TPU:1, one launch (start us, length us, event | category | flops | bytes accessed | tf_op | source)
XLA Modules:
  0.0 65.0 jit_solution(668832045117866606)
XLA Ops:
  0.6 62.9 %shard_map.131 = (bf16[256,256]{1,0:T(8,128)(2,1)S(1)}, bf16[256,256]{1,0:T(8,128)(2,1)S(1)}, bf16[512,512]{1,0:T(8,128)(2,1)S(1)}, bf16[512,512]{1,0:T(8,128)(2,1)S(1)}, bf16[2,64,64,128]{3,2,1,0:T(8,128)(2,1)S(1)}) custom-call(f32[16,8,1024]{2,1,0:T(8,128)} %field_hbm.1, bf16[2,64,64,128]{3,2,1,0:T(8,128)(2,1)} %weights_hbm.1, f32[16,4,512]{2,1,0:T(4,128)} %cot_hbm.1, ...), custom_call_target="tpu_custom_call" | custom-call | tf_op jit(solution)/shard_map/pallas_call | solution.py:336
  63.5 1.5 %shard_map.132 = (bf16[16,8,1024]{2,1,0:T(8,128)(2,1)}, bf16[2,64,64,128]{3,2,1,0:T(8,128)(2,1)}) custom-call(bf16[256,256]{1,0:T(8,128)(2,1)S(1)} %get-tuple-element.7.left_h, bf16[256,256]{1,0:T(8,128)(2,1)S(1)} %get-tuple-element.8.left_l, bf16[512,512]{1,0:T(8,128)(2,1)S(1)} %get-tuple-element.9.t1h, bf16[512,512]{1,0:T(8,128)(2,1)S(1)} %get-tuple-element.10.t1l, ...), custom_call_target="tpu_custom_call" | custom-call | tf_op jit(solution)/shard_map/pallas_call | solution.py:368

commit v4 on v3

--- a/solution.py
+++ b/solution.py
@@ -84,7 +84,7 @@
     left_h, left_l, t1h, t1l, gweights,
     field, weights, cot, t4h, t4l, wah, wal, wbh, wbl, twiddle,
     send1, recv1, send2, recv2, send3, recv3, send4, recv4,
-    csend, crecv, mixed, part_r, part_i, back_r, back_i,
+    csend, crecv, mixed, part_r, part_i,
     in_sem, row_send, row_recv, chan_send, chan_recv,
 ):
     me = lax.axis_index("rows")
@@ -211,7 +211,7 @@
             wr, wi = weights[0, channel].astype(jnp.float32), weights[1, channel].astype(jnp.float32)
             return out_r + (xr * wr - xi * wi), out_i + (xr * wi + xi * wr)
 
-        return lax.fori_loop(0, 16, step, carry, unroll=4)
+        return lax.fori_loop(0, 16, step, carry, unroll=8)
 
     zero = jnp.zeros((64, 128), jnp.float32)
     total = (zero, zero)
@@ -265,14 +265,13 @@
 
     def unmix(i, _):
         real, imag = terms(crecv, 1 - core, i)
-        back_r[pl.ds(i, 1), :] = jnp.sum(part_r[i] + real, axis=0, keepdims=True)
-        back_i[pl.ds(i, 1), :] = jnp.sum(part_i[i] + imag, axis=0, keepdims=True)
+        part_r[i], part_i[i] = part_r[i] + real, part_i[i] + imag
         return 0
 
-    lax.fori_loop(0, 64, unmix_own, 0, unroll=4)
+    lax.fori_loop(0, 64, unmix_own, 0, unroll=8)
     swap(2).wait_recv()
-    lax.fori_loop(0, 64, unmix, 0, unroll=4)
-    give_modes(3, back_r, back_i)
+    lax.fori_loop(0, 64, unmix, 0, unroll=8)
+    give_modes(3, *(sum(part[:, u, :] for u in range(8)) for part in (part_r, part_i)))
     swap(3).wait_recv()
 
     tall = from_modes(3, HL, 0)
@@ -354,7 +353,6 @@
             pltpu.VMEM((4, 2, 2, 32, 128), f32),
             pltpu.VMEM((4, 128, 128), f32),
             *[pltpu.VMEM((64, 8, 128), f32)] * 2,
-            *[pltpu.VMEM((64, 128), f32)] * 2,
             pltpu.SemaphoreType.DMA((12,)),
             pltpu.SemaphoreType.DMA((4,)),
             pltpu.SemaphoreType.DMA((4,)),

time: 65.4 us -> 65.2 us (level)
  no operation moved by 1% of the time
where the time goes in v4:
time: 65.2 us; the launch traced here: 64.8 us
  Pallas kernels  64.2 us (98%)
    pallas_call x1, Pallas kernels, local(): pl.pallas_call(kernel, out_shape=(pltpu.VMEM((256, 256), bf16), pltpu.VME...  62.7 us
    pallas_call x1, Pallas kernels, local(): pl.pallas_call(finish, out_shape=(jax.ShapeDtypeStruct(field.shape, bf16)...  1.48 us

profile of v4, /device:TPU:1, one launch (start us, length us, event | category | flops | bytes accessed | tf_op | source)
XLA Modules:
  0.0 64.8 jit_solution(6123620390902937386)
XLA Ops:
  0.6 62.7 %shard_map.131 = (bf16[256,256]{1,0:T(8,128)(2,1)S(1)}, bf16[256,256]{1,0:T(8,128)(2,1)S(1)}, bf16[512,512]{1,0:T(8,128)(2,1)S(1)}, bf16[512,512]{1,0:T(8,128)(2,1)S(1)}, bf16[2,64,64,128]{3,2,1,0:T(8,128)(2,1)S(1)}) custom-call(f32[16,8,1024]{2,1,0:T(8,128)} %field_hbm.1, bf16[2,64,64,128]{3,2,1,0:T(8,128)(2,1)} %weights_hbm.1, f32[16,4,512]{2,1,0:T(4,128)} %cot_hbm.1, ...), custom_call_target="tpu_custom_call" | custom-call | tf_op jit(solution)/shard_map/pallas_call | solution.py:335
  63.4 1.5 %shard_map.132 = (bf16[16,8,1024]{2,1,0:T(8,128)(2,1)}, bf16[2,64,64,128]{3,2,1,0:T(8,128)(2,1)}) custom-call(bf16[256,256]{1,0:T(8,128)(2,1)S(1)} %get-tuple-element.7.left_h, bf16[256,256]{1,0:T(8,128)(2,1)S(1)} %get-tuple-element.8.left_l, bf16[512,512]{1,0:T(8,128)(2,1)S(1)} %get-tuple-element.9.t1h, bf16[512,512]{1,0:T(8,128)(2,1)S(1)} %get-tuple-element.10.t1l, ...), custom_call_target="tpu_custom_call" | custom-call | tf_op jit(solution)/shard_map/pallas_call | solution.py:366
